TPU v7x, 512 devices: a whole 4x4x16 slice. The times are simulated.
512 devices in a mesh: expert: 64 (over z, x), tensor: 8 (over y, core).
Axes of the slice: x: 4, y: 4, z: 16, core: 2. Of those that a mesh axis runs over, the one named last changes fastest.
Arguments:
- tokens: bfloat16 [8192, 2048], P(('expert', 'tensor')), may hold values from -40 to 40
- cotangent: bfloat16 [8192, 2048], P(('expert', 'tensor')), may hold values from -32 to 32
- gain: float32 [2048], replicated, may hold values from 0.1 to 1.9
- expert_ids: int32 [8192, 8], P('expert'), may hold values from 0 to 127, all different within a row; in each aligned block of 128 rows (0 to 127, 128 to 255, ...) at most 12 rows name the same one
- gate_probs: float32 [8192, 8], P('expert'), may hold values from 0.05 to 0.3
- gate_up_weight: bfloat16 [512, 2048, 384], P(('expert', 'tensor')), may hold values from -0.125 to 0.125
- down_weight: bfloat16 [512, 192, 2048], P(('expert', 'tensor')), may hold values from -0.21875 to 0.21875
Outputs:
- mixed: bfloat16 [8192, 2048], P(('expert', 'tensor'))
- token_grad: bfloat16 [8192, 2048], P(('expert', 'tensor'))
- prob_grad: float32 [8192, 8], P(('expert', 'tensor'))
- gain_grad: float32 [2048], replicated
- gate_up_grad: bfloat16 [512, 2048, 384], P(('expert', 'tensor'))
- down_grad: bfloat16 [512, 192, 2048], P(('expert', 'tensor'))
Inputs may be any that keep to these rules, and one draw needn't show every extreme that they name: `expert_ids`: in each aligned block of 128 rows, the tokens of one index of the expert axis, no expert is named by more than 12 rows.
All inputs are finite; a program needn't handle non-finite values.
Results may differ from a plain program's by a relative error of at most 0.009.
Values may be sent and summed in bfloat16 or wider, within the bound.
A program may use at most 128 MiB of HBM per device.

v0:
```python
import jax
import jax.numpy as jnp
from jax import lax
from jax.sharding import PartitionSpec as P

TOP = 8
EXP_DEV = 2


def normalize(rows):
    values = rows.astype(jnp.float32)
    inv_rms = lax.rsqrt(jnp.mean(values * values, axis=1, keepdims=True) + 1e-06)
    return (values * inv_rms, inv_rms)


def expert_forward(rows, gate_up, down_proj):
    projected = jnp.dot(rows, gate_up, preferred_element_type=jnp.float32)
    half_width = down_proj.shape[0]
    gate_pre = projected[:, :half_width]
    up_pre = projected[:, half_width:]
    sigmoid_gate = jax.nn.sigmoid(gate_pre)
    hidden = (gate_pre * sigmoid_gate * up_pre).astype(jnp.bfloat16)
    block_out = jnp.dot(hidden, down_proj, preferred_element_type=jnp.float32).astype(jnp.bfloat16)
    return (gate_pre, up_pre, sigmoid_gate, hidden, block_out)


def expert_backward(rows, slot_grads, gate_up, down_proj, gate_pre, up_pre, sigmoid_gate, hidden):
    hidden_grad = lax.dot_general(
        slot_grads, down_proj, (((1,), (1,)), ((), ())), preferred_element_type=jnp.float32
    )
    gate_grad = (
        hidden_grad * up_pre * sigmoid_gate * (1.0 + gate_pre * (1.0 - sigmoid_gate))
    ).astype(jnp.bfloat16)
    up_grad = (hidden_grad * gate_pre * sigmoid_gate).astype(jnp.bfloat16)
    joined_grad = jnp.concatenate([gate_grad, up_grad], axis=1)
    down_part = lax.dot_general(
        hidden, slot_grads, (((0,), (0,)), ((), ())), preferred_element_type=jnp.float32
    ).astype(jnp.bfloat16)
    gate_up_part = lax.dot_general(
        rows, joined_grad, (((0,), (0,)), ((), ())), preferred_element_type=jnp.float32
    ).astype(jnp.bfloat16)
    input_grad = lax.dot_general(
        joined_grad, gate_up, (((1,), (1,)), ((), ())), preferred_element_type=jnp.float32
    ).astype(jnp.bfloat16)
    return (input_grad, gate_up_part, down_part)


def shards(tokens, cotangent, gain, expert_ids, gate_probs, gate_up_weight, down_weight):
    tensor_size = lax.axis_size("tensor")
    expert_size = lax.axis_size("expert")
    my_rank = lax.axis_index("tensor")
    blocks_each = tensor_size // EXP_DEV
    my_type = my_rank // blocks_each
    group_rows = expert_ids.shape[0]
    features = tokens.shape[1]
    capacity = 3 * group_rows * TOP // (2 * EXP_DEV * expert_size)
    highest = lax.Precision.HIGHEST
    scaled_own, inv_own = normalize(tokens)
    carried = (scaled_own * gain[None, :]).astype(jnp.bfloat16)
    group_first, group_grads = (
        lax.all_gather(carried, "tensor", axis=0, tiled=True),
        lax.all_gather(cotangent, "tensor", axis=0, tiled=True),
    )
    targets = jnp.arange(expert_size, dtype=jnp.int32) * EXP_DEV + my_type
    matches = expert_ids[:, :, None] == targets[None, None, :]
    chosen = jnp.any(matches, axis=1)
    weight_of = jnp.sum(jnp.where(matches, gate_probs[:, :, None], 0.0), axis=1)
    slot_of = jnp.sum(
        jnp.where(matches, jnp.arange(TOP, dtype=jnp.int32)[None, :, None], 0), axis=1
    )
    row_ids = jnp.arange(group_rows, dtype=jnp.int32)
    earlier = (row_ids[None, :] < row_ids[:, None]).astype(jnp.bfloat16)
    rank_in = jnp.dot(
        earlier, chosen.astype(jnp.bfloat16), preferred_element_type=jnp.float32
    ).astype(jnp.int32)
    placed = chosen.T[:, None, :] & (
        rank_in.T[:, None, :] == jnp.arange(capacity, dtype=jnp.int32)[None, :, None]
    )
    source = jnp.sum(jnp.where(placed, row_ids[None, None, :], 0), axis=2)
    filled = jnp.any(placed, axis=2)
    slot_prob = jnp.sum(jnp.where(placed, weight_of.T[:, None, :], 0.0), axis=2)
    slot_index = jnp.sum(jnp.where(placed, slot_of.T[:, None, :], 0), axis=2)
    sent_rows = jnp.where(
        filled[:, :, None], jnp.take(group_first, source, axis=0), jnp.zeros((), jnp.bfloat16)
    )
    sent_grads = (
        slot_prob[:, :, None] * jnp.take(group_grads, source, axis=0).astype(jnp.float32)
    ).astype(jnp.bfloat16)
    gate_up = gate_up_weight[0]
    down_proj = down_weight[0]
    arrived_rows, arrived_grads = (
        lax.all_to_all(sent_rows, "expert", split_axis=0, concat_axis=0, tiled=True),
        lax.all_to_all(sent_grads, "expert", split_axis=0, concat_axis=0, tiled=True),
    )
    rows = arrived_rows.reshape(-1, features)
    slot_grads = arrived_grads.reshape(-1, features)
    gate_pre, up_pre, sigmoid_gate, hidden, block_out = expert_forward(rows, gate_up, down_proj)
    out_slots = block_out.reshape(expert_size, capacity, features)
    input_grad, gate_up_part, down_part = expert_backward(
        rows, slot_grads, gate_up, down_proj, gate_pre, up_pre, sigmoid_gate, hidden
    )
    input_slots = input_grad.reshape(expert_size, capacity, features)
    out_back, input_back = (
        lax.all_to_all(out_slots, "expert", split_axis=0, concat_axis=0, tiled=True),
        lax.all_to_all(input_slots, "expert", split_axis=0, concat_axis=0, tiled=True),
    )
    out_flat = out_back.reshape(-1, features)
    input_flat = input_back.reshape(-1, features)
    used_source = source.reshape(-1)
    used_filled = filled.reshape(-1)
    used_prob = slot_prob.reshape(-1)
    used_index = slot_index.reshape(-1)
    cot_slots = jnp.take(group_grads, used_source, axis=0)
    prob_values = jnp.einsum("sd,sd->s", cot_slots, out_flat, preferred_element_type=jnp.float32)
    hit = (row_ids[:, None] == used_source[None, :]) & used_filled[None, :]
    input_part = jnp.dot(hit.astype(jnp.bfloat16), input_flat, preferred_element_type=jnp.float32)
    weighting = jnp.where(hit, used_prob[None, :], 0.0)
    out_part = jnp.dot(
        weighting,
        out_flat.astype(jnp.float32),
        precision=highest,
        preferred_element_type=jnp.float32,
    )
    prob_columns = jnp.where(
        used_index[:, None] == jnp.arange(TOP, dtype=jnp.int32)[None, :], prob_values[:, None], 0.0
    )
    prob_part = jnp.dot(
        hit.astype(jnp.float32), prob_columns, precision=highest, preferred_element_type=jnp.float32
    )
    out_sum, normed_grad, prob_grad = (
        lax.psum_scatter(out_part, "tensor", scatter_dimension=0, tiled=True),
        lax.psum_scatter(input_part, "tensor", scatter_dimension=0, tiled=True),
        lax.psum_scatter(prob_part, "tensor", scatter_dimension=0, tiled=True),
    )
    mixed = (tokens.astype(jnp.float32) + out_sum).astype(jnp.bfloat16)
    gain_side = normed_grad * gain[None, :]
    token_grad = (
        cotangent.astype(jnp.float32)
        + inv_own
        * (gain_side - scaled_own * jnp.mean(gain_side * scaled_own, axis=1, keepdims=True))
    ).astype(jnp.bfloat16)
    gain_grad = lax.psum(jnp.sum(normed_grad * scaled_own, axis=0), ("expert", "tensor"))
    return (mixed, token_grad, prob_grad, gain_grad, gate_up_part[None], down_part[None])


def solution(mesh):
    in_specs = (
        P(("expert", "tensor"), None),
        P(("expert", "tensor"), None),
        P(),
        P("expert", None),
        P("expert", None),
        P(("expert", "tensor"), None, None),
        P(("expert", "tensor"), None, None),
    )
    out_specs = (
        P(("expert", "tensor"), None),
        P(("expert", "tensor"), None),
        P(("expert", "tensor"), None),
        P(),
        P(("expert", "tensor"), None, None),
        P(("expert", "tensor"), None, None),
    )
    return jax.shard_map(shards, mesh=mesh, in_specs=in_specs, out_specs=out_specs, check_vma=False)
```

profile of v0, /device:TPU:1, one launch (start us, length us, event | category | flops | bytes accessed | tf_op | source)
XLA Modules:
  0.0 1010.0 jit_solution(2385473956684537475)
XLA Ops:
  12.2 19.8 %all_gather.6 = bf16[128,2048]{1,0:T(8,128)(2,1)S(1)} all-gather(bf16[16,2048]{1,0:T(8,128)(2,1)S(1)} %fusion.37), channel_id=1, replica_groups=mesh['expert'=64,'tensor'=8] {'tensor'}, dimensions={0}, use_global_device_ids=true | all-gather | bytes 589824 | tf_op jit(solution)/shard_map/all_gather | solution.py:61
  36.3 6.1 reshape.141
  46.3 13.8 %all-to-all-start = ((bf16[64,12,2048]{2,1,0:T(8,128)(2,1)}), bf16[64,12,2048]{2,1,0:T(8,128)(2,1)}, u32[]{:S(2)}, u32[]{:S(2)}) async-start(bf16[64,12,2048]{2,1,0:T(8,128)(2,1)} %select_select_fusion), calls=%async_computation | async-start | bytes 8388608 | tf_op jit(solution)/shard_map/all_to_all | solution.py:92
  60.5 13.4 %all_gather.7 = bf16[128,2048]{1,0:T(8,128)(2,1)S(1)} all-gather(bf16[16,2048]{1,0:T(8,128)(2,1)S(1)} %copy-done.4), channel_id=1, replica_groups=mesh['expert'=64,'tensor'=8] {'tensor'}, dimensions={0}, use_global_device_ids=true | all-gather | bytes 589824 | tf_op jit(solution)/shard_map/all_gather | solution.py:62
  73.9 4.3 gather_fusion.2
  78.2 6.1 reshape.145
  88.5 155.2 %all-to-all-done = bf16[64,12,2048]{2,1,0:T(8,128)(2,1)} async-done(((bf16[64,12,2048]{2,1,0:T(8,128)(2,1)}), bf16[64,12,2048]{2,1,0:T(8,128)(2,1)}, u32[]{:S(2)}, u32[]{:S(2)}) %all-to-all-start) | async-done | bytes 3145760 | tf_op jit(solution)/shard_map/all_to_all | solution.py:92
  243.6 12.1 %all-to-all-start.2 = ((bf16[64,12,2048]{2,1,0:T(8,128)(2,1)}), bf16[64,12,2048]{2,1,0:T(8,128)(2,1)}, u32[]{:S(2)}, u32[]{:S(2)}) async-start(bf16[64,12,2048]{2,1,0:T(8,128)(2,1)} %multiply_convert_fusion), calls=%async_computation.3 | async-start | bytes 8388608 | tf_op jit(solution)/shard_map/all_to_all | solution.py:93
  255.7 6.2 reshape.103
  261.9 4.3 fusion.4
  266.2 173.2 %all-to-all-done.2 = bf16[64,12,2048]{2,1,0:T(8,128)(2,1)} async-done(((bf16[64,12,2048]{2,1,0:T(8,128)(2,1)}), bf16[64,12,2048]{2,1,0:T(8,128)(2,1)}, u32[]{:S(2)}, u32[]{:S(2)}) %all-to-all-start.2) | async-done | bytes 3145760 | tf_op jit(solution)/shard_map/all_to_all | solution.py:93
  439.4 6.2 reshape.106
  445.6 4.3 multiply_convert_fusion.2
  452.6 6.1 reshape.104
  458.7 11.9 %all-to-all-start.1 = ((bf16[64,12,2048]{2,1,0:T(8,128)(2,1)}), bf16[64,12,2048]{2,1,0:T(8,128)(2,1)}, u32[]{:S(2)}, u32[]{:S(2)}) async-start(bf16[64,12,2048]{2,1,0:T(8,128)(2,1)} %reshape.104), calls=%async_computation.1 | async-start | bytes 8388608 | tf_op jit(solution)/shard_map/all_to_all | solution.py:104
  474.1 6.1 reshape.107
  480.2 173.7 %all-to-all-done.1 = bf16[64,12,2048]{2,1,0:T(8,128)(2,1)} async-done(((bf16[64,12,2048]{2,1,0:T(8,128)(2,1)}), bf16[64,12,2048]{2,1,0:T(8,128)(2,1)}, u32[]{:S(2)}, u32[]{:S(2)}) %all-to-all-start.1) | async-done | bytes 3145760 | tf_op jit(solution)/shard_map/all_to_all | solution.py:104
  654.0 11.9 %all-to-all-start.3 = ((bf16[64,12,2048]{2,1,0:T(8,128)(2,1)}), bf16[64,12,2048]{2,1,0:T(8,128)(2,1)}, u32[]{:S(2)}, u32[]{:S(2)}) async-start(bf16[64,12,2048]{2,1,0:T(8,128)(2,1)} %reshape.107), calls=%async_computation.4 | async-start | bytes 8388608 | tf_op jit(solution)/shard_map/all_to_all | solution.py:105
  670.9 6.2 reshape.105
  682.3 167.0 %all-to-all-done.3 = bf16[64,12,2048]{2,1,0:T(8,128)(2,1)} async-done(((bf16[64,12,2048]{2,1,0:T(8,128)(2,1)}), bf16[64,12,2048]{2,1,0:T(8,128)(2,1)}, u32[]{:S(2)}, u32[]{:S(2)}) %all-to-all-start.3) | async-done | bytes 3145760 | tf_op jit(solution)/shard_map/all_to_all | solution.py:105
  849.3 6.2 reshape.108
  859.1 4.3 fusion.11
  871.6 23.3 %reduce-scatter.8.cloned.1.call-done = f32[16,2048]{1,0:T(8,128)} async-done(((f32[128,2048]{1,0:T(8,128)}), f32[16,2048]{1,0:T(8,128)}) %reduce-scatter.8.cloned.1.call-update) | async-done | bytes 131088 | tf_op jit(solution)/shard_map/reduce_scatter | solution.py:132
  896.0 105.8 %psum.7 = f32[2048]{0:T(1024)} all-reduce(f32[2048]{0:T(1024)S(1)} %get-tuple-element.7), channel_id=1, replica_groups=mesh['expert'=64,'tensor'=8] {'expert','tensor'}, use_global_device_ids=true, to_apply=%region_13.15 | all-reduce | flops 2048 | bytes 16384 | tf_op jit(solution)/shard_map/psum | solution.py:142
  (72 shorter events, 48.7 us)
Async XLA Ops:
  7.2 254.7 %copy-start = (bf16[1,2048,384]{2,1,0:T(8,128)(2,1)S(1)}, bf16[1,2048,384]{2,1,0:T(8,128)(2,1)}, u32[]{:S(2)}) copy-start(bf16[1,2048,384]{2,1,0:T(8,128)(2,1)} %param.14) | copy-start | bytes 4718596
  46.3 13.8 %copy-start.6 = (s32[128,8]{0,1:T(8,128)S(1)}, s32[128,8]{0,1:T(8,128)}, u32[]{:S(2)}) copy-start(s32[128,8]{0,1:T(8,128)} %param.12) | copy-start | bytes 12292
  46.3 13.9 %copy-start.7 = (f32[128,8]{0,1:T(8,128)S(1)}, f32[128,8]{0,1:T(8,128)}, u32[]{:S(2)}) copy-start(f32[128,8]{0,1:T(8,128)} %param.13) | copy-start | bytes 12292
  46.3 14.2 %copy-start.4 = (bf16[16,2048]{1,0:T(8,128)(2,1)S(1)}, bf16[16,2048]{1,0:T(8,128)(2,1)}, u32[]{:S(2)}) copy-start(bf16[16,2048]{1,0:T(8,128)(2,1)} %param.10) | copy-start | bytes 196612
  46.3 197.3 %all-to-all-start = ((bf16[64,12,2048]{2,1,0:T(8,128)(2,1)}), bf16[64,12,2048]{2,1,0:T(8,128)(2,1)}, u32[]{:S(2)}, u32[]{:S(2)}) async-start(bf16[64,12,2048]{2,1,0:T(8,128)(2,1)} %select_select_fusion), calls=%async_computation | async-start | bytes 8388608 | tf_op jit(solution)/shard_map/all_to_all | solution.py:92
  243.6 195.8 %all-to-all-start.2 = ((bf16[64,12,2048]{2,1,0:T(8,128)(2,1)}), bf16[64,12,2048]{2,1,0:T(8,128)(2,1)}, u32[]{:S(2)}, u32[]{:S(2)}) async-start(bf16[64,12,2048]{2,1,0:T(8,128)(2,1)} %multiply_convert_fusion), calls=%async_computation.3 | async-start | bytes 8388608 | tf_op jit(solution)/shard_map/all_to_all | solution.py:93
  266.2 179.4 %copy-start.3 = (bf16[1,192,2048]{2,1,0:T(8,128)(2,1)S(1)}, bf16[1,192,2048]{2,1,0:T(8,128)(2,1)}, u32[]{:S(2)}) copy-start(bf16[1,192,2048]{2,1,0:T(8,128)(2,1)} %param.15) | copy-start | bytes 2359300
  458.7 11.9 %copy-start.8 = (bf16[768,192]{0,1:T(8,128)(2,1)S(1)}, bf16[768,192]{0,1:T(8,128)(2,1)}, u32[]{:S(2)}) copy-start(bf16[768,192]{0,1:T(8,128)(2,1)} %get-tuple-element.11) | copy-start | bytes 884740
  458.7 11.9 %copy-start.9 = (bf16[768,192]{0,1:T(8,128)(2,1)S(1)}, bf16[768,192]{0,1:T(8,128)(2,1)}, u32[]{:S(2)}) copy-start(bf16[768,192]{0,1:T(8,128)(2,1)} %get-tuple-element.12) | copy-start | bytes 884740
  458.7 195.3 %all-to-all-start.1 = ((bf16[64,12,2048]{2,1,0:T(8,128)(2,1)}), bf16[64,12,2048]{2,1,0:T(8,128)(2,1)}, u32[]{:S(2)}, u32[]{:S(2)}) async-start(bf16[64,12,2048]{2,1,0:T(8,128)(2,1)} %reshape.104), calls=%async_computation.1 | async-start | bytes 8388608 | tf_op jit(solution)/shard_map/all_to_all | solution.py:104
  654.0 195.3 %all-to-all-start.3 = ((bf16[64,12,2048]{2,1,0:T(8,128)(2,1)}), bf16[64,12,2048]{2,1,0:T(8,128)(2,1)}, u32[]{:S(2)}, u32[]{:S(2)}) async-start(bf16[64,12,2048]{2,1,0:T(8,128)(2,1)} %reshape.107), calls=%async_computation.4 | async-start | bytes 8388608 | tf_op jit(solution)/shard_map/all_to_all | solution.py:105
  665.9 204.3 %reduce-scatter.10.cloned.1.call-start = ((), (), s32[]{:S(2)}) async-start(), calls=%async_computation.9 | async-start | bytes 73728
  682.2 212.6 %reduce-scatter.8.cloned.1.call-start = ((), (), s32[]{:S(2)}) async-start(), calls=%async_computation.8 | async-start | bytes 1179648 | tf_op jit(solution)/shard_map/reduce_scatter | solution.py:132
  858.9 142.8 %reduce-scatter.6.cloned.1.call-start = ((), (), s32[]{:S(2)}) async-start(), calls=%async_computation.7 | async-start | bytes 1179648 | tf_op jit(solution)/shard_map/reduce_scatter | solution.py:131
  863.4 3.7 copy-start.1
  867.2 27.7 %copy-start.2 = (bf16[16,2048]{1,0:T(8,128)(2,1)S(1)}, bf16[16,2048]{1,0:T(8,128)(2,1)}, u32[]{:S(2)}) copy-start(bf16[16,2048]{1,0:T(8,128)(2,1)} %param.9) | copy-start | bytes 196612
  867.2 27.7 %copy-start.5 = (f32[2048]{0:T(1024)S(1)}, f32[2048]{0:T(1024)}, u32[]{:S(2)}) copy-start(f32[2048]{0:T(1024)} %param.11) | copy-start | bytes 24580
Sparse Core Ops, SparseCore 0:
  682.4 38.4 reduce-scatter.9
  859.1 35.7 reduce-scatter.7
  897.9 38.6 reduce-scatter.5
where the time goes:
time: 1010 us
  waiting for transfers between devices  692 us (69%)
  blocking collectives  139 us (14%)
  local copies, waits for them, and re-layouts  64.5 us (6%)
  starting transfers between devices  49.8 us (5%)
  matrix products  30.7 us (3%)
  other arithmetic  19.6 us (2%)
  between operations  14 us (1%)
    all_to_all x1, waiting for transfers between devices, shards(): lax.all_to_all(out_slots, 'expert', split_axis=0, concat_axis=0, tiled=True)  174 us
    all_to_all x1, waiting for transfers between devices, shards(): lax.all_to_all(sent_grads, 'expert', split_axis=0, concat_axis=0, tiled=T...  173 us
    all_to_all x1, waiting for transfers between devices, shards(): lax.all_to_all(input_slots, 'expert', split_axis=0, concat_axis=0, tiled=...  167 us
    all_to_all x1, waiting for transfers between devices, shards(): lax.all_to_all(sent_rows, 'expert', split_axis=0, concat_axis=0, tiled=True)  155 us
    psum x1, blocking collectives, shards(): lax.psum(jnp.sum(normed_grad * scaled_own, axis=0), ('expert', 'tensor'))  106 us
    reduce_scatter x1, waiting for transfers between devices, shards(): lax.psum_scatter(input_part, 'tensor', scatter_dimension=0, tiled=True)  23.3 us
  transfers between devices with their start and end apart: 7, of which 5 were waited for; matrix products, arithmetic and copies ran while one was open for 7% of the time, Pallas kernels for 0%

commit v1 on v0

--- a/solution.py
+++ b/solution.py
@@ -139,7 +139,9 @@
         + inv_own
         * (gain_side - scaled_own * jnp.mean(gain_side * scaled_own, axis=1, keepdims=True))
     ).astype(jnp.bfloat16)
-    gain_grad = lax.psum(jnp.sum(normed_grad * scaled_own, axis=0), ("expert", "tensor"))
+    gain_grad = jnp.sum(
+        lax.all_gather(jnp.sum(normed_grad * scaled_own, axis=0), ("expert", "tensor")), axis=0
+    )
     return (mixed, token_grad, prob_grad, gain_grad, gate_up_part[None], down_part[None])
 
 

time: 1010 us -> 1160 us (1.15)
  waiting for transfers between devices: 692 us -> 938 us
  blocking collectives: 139 us -> 33.2 us
    all_gather x0 -> x1, waiting for transfers between devices: none -> 203 us  [shards(): lax.all_gather(jnp.sum(normed_grad * scaled_own, axis=0), ('expert', 'ten...]
    psum x1 -> x0, blocking collectives: 106 us -> none  [shards(): lax.psum(jnp.sum(normed_grad * scaled_own, axis=0), ('expert', 'tensor'))]
    reduce_scatter x1, waiting for transfers between devices: 0.01 us -> 40.1 us  [shards(): lax.psum_scatter(out_part, 'tensor', scatter_dimension=0, tiled=True)]
    reduce_scatter x1, waiting for transfers between devices: 23.3 us -> 0.02 us  [shards(): lax.psum_scatter(input_part, 'tensor', scatter_dimension=0, tiled=True)]
    unnamed x4 -> x5, waiting for transfers between devices: 0.05 us -> 23.1 us
  transfers between devices with their start and end apart: 7 -> 8, of which waited for: 5 -> 7; matrix products, arithmetic and copies ran while one was open for 7% -> 6% of each run, Pallas kernels for 0% -> 0%
where the time goes in v1:
time: 1160 us; the launch traced here: 1150 us
  waiting for transfers between devices  938 us (81%)
  local copies, waits for them, and re-layouts  68.9 us (6%)
  starting transfers between devices  49.6 us (4%)
  blocking collectives  33.2 us (3%)
  matrix products  27.9 us (2%)
  other arithmetic  22.2 us (2%)
  between operations  14.1 us (1%)
    all_gather x1, waiting for transfers between devices, shards(): lax.all_gather(jnp.sum(normed_grad * scaled_own, axis=0), ('expert', 'ten...  203 us
    all_to_all x1, waiting for transfers between devices, shards(): lax.all_to_all(input_slots, 'expert', split_axis=0, concat_axis=0, tiled=...  175 us
    all_to_all x1, waiting for transfers between devices, shards(): lax.all_to_all(sent_grads, 'expert', split_axis=0, concat_axis=0, tiled=T...  173 us
    all_to_all x1, waiting for transfers between devices, shards(): lax.all_to_all(out_slots, 'expert', split_axis=0, concat_axis=0, tiled=True)  169 us
    all_to_all x1, waiting for transfers between devices, shards(): lax.all_to_all(sent_rows, 'expert', split_axis=0, concat_axis=0, tiled=True)  155 us
    reduce_scatter x1, waiting for transfers between devices, shards(): lax.psum_scatter(out_part, 'tensor', scatter_dimension=0, tiled=True)  40.1 us
  transfers between devices with their start and end apart: 8, of which 7 were waited for; matrix products, arithmetic and copies ran while one was open for 6% of the time, Pallas kernels for 0%

profile of v1, /device:TPU:1, one launch (start us, length us, event | category | flops | bytes accessed | tf_op | source)
XLA Modules:
  0.0 1153.8 jit_solution(7208189177416348533)
XLA Ops:
  12.2 19.8 %all_gather.12 = bf16[128,2048]{1,0:T(8,128)(2,1)S(1)} all-gather(bf16[16,2048]{1,0:T(8,128)(2,1)S(1)} %fusion.37), channel_id=1, replica_groups=mesh['expert'=64,'tensor'=8] {'tensor'}, dimensions={0}, use_global_device_ids=true | all-gather | bytes 589824 | tf_op jit(solution)/shard_map/all_gather | solution.py:61
  36.3 6.1 reshape.142
  46.3 13.8 %all-to-all-start = ((bf16[64,12,2048]{2,1,0:T(8,128)(2,1)}), bf16[64,12,2048]{2,1,0:T(8,128)(2,1)}, u32[]{:S(2)}, u32[]{:S(2)}) async-start(bf16[64,12,2048]{2,1,0:T(8,128)(2,1)} %select_select_fusion), calls=%async_computation | async-start | bytes 8388608 | tf_op jit(solution)/shard_map/all_to_all | solution.py:92
  60.5 13.4 %all_gather.13 = bf16[128,2048]{1,0:T(8,128)(2,1)S(1)} all-gather(bf16[16,2048]{1,0:T(8,128)(2,1)S(1)} %copy-done.6), channel_id=1, replica_groups=mesh['expert'=64,'tensor'=8] {'tensor'}, dimensions={0}, use_global_device_ids=true | all-gather | bytes 589824 | tf_op jit(solution)/shard_map/all_gather | solution.py:62
  78.2 6.1 reshape.146
  88.5 155.2 %all-to-all-done = bf16[64,12,2048]{2,1,0:T(8,128)(2,1)} async-done(((bf16[64,12,2048]{2,1,0:T(8,128)(2,1)}), bf16[64,12,2048]{2,1,0:T(8,128)(2,1)}, u32[]{:S(2)}, u32[]{:S(2)}) %all-to-all-start) | async-done | bytes 3145760 | tf_op jit(solution)/shard_map/all_to_all | solution.py:92
  243.6 12.3 %all-to-all-start.2 = ((bf16[64,12,2048]{2,1,0:T(8,128)(2,1)}), bf16[64,12,2048]{2,1,0:T(8,128)(2,1)}, u32[]{:S(2)}, u32[]{:S(2)}) async-start(bf16[64,12,2048]{2,1,0:T(8,128)(2,1)} %multiply_convert_fusion), calls=%async_computation.3 | async-start | bytes 8388608 | tf_op jit(solution)/shard_map/all_to_all | solution.py:93
  255.9 6.2 reshape.103
  262.1 4.3 fusion.4
  266.4 173.3 %all-to-all-done.2 = bf16[64,12,2048]{2,1,0:T(8,128)(2,1)} async-done(((bf16[64,12,2048]{2,1,0:T(8,128)(2,1)}), bf16[64,12,2048]{2,1,0:T(8,128)(2,1)}, u32[]{:S(2)}, u32[]{:S(2)}) %all-to-all-start.2) | async-done | bytes 3145760 | tf_op jit(solution)/shard_map/all_to_all | solution.py:93
  439.7 6.2 reshape.106
  453.8 6.1 reshape.107
  459.8 11.3 all-to-all-start.3
  473.8 6.1 reshape.104
  479.9 174.6 %all-to-all-done.3 = bf16[64,12,2048]{2,1,0:T(8,128)(2,1)} async-done(((bf16[64,12,2048]{2,1,0:T(8,128)(2,1)}), bf16[64,12,2048]{2,1,0:T(8,128)(2,1)}, u32[]{:S(2)}, u32[]{:S(2)}) %all-to-all-start.3) | async-done | bytes 3145760 | tf_op jit(solution)/shard_map/all_to_all | solution.py:105
  654.5 11.9 %all-to-all-start.1 = ((bf16[64,12,2048]{2,1,0:T(8,128)(2,1)}), bf16[64,12,2048]{2,1,0:T(8,128)(2,1)}, u32[]{:S(2)}, u32[]{:S(2)}) async-start(bf16[64,12,2048]{2,1,0:T(8,128)(2,1)} %reshape.104), calls=%async_computation.1 | async-start | bytes 8388608 | tf_op jit(solution)/shard_map/all_to_all | solution.py:104
  666.8 6.2 reshape.108
  676.9 4.3 gather_fusion
  681.3 168.6 %all-to-all-done.1 = bf16[64,12,2048]{2,1,0:T(8,128)(2,1)} async-done(((bf16[64,12,2048]{2,1,0:T(8,128)(2,1)}), bf16[64,12,2048]{2,1,0:T(8,128)(2,1)}, u32[]{:S(2)}, u32[]{:S(2)}) %all-to-all-start.1) | async-done | bytes 3145760 | tf_op jit(solution)/shard_map/all_to_all | solution.py:104
  849.8 4.7 reshape.105
  870.1 23.0 %reduce-scatter.10.cloned.1.call-done = f32[16,8]{1,0:T(8,128)} async-done(((f32[128,8]{1,0:T(8,128)}), f32[16,8]{1,0:T(8,128)}) %reduce-scatter.10.cloned.1.call-update) | async-done | bytes 528
  894.5 40.1 %reduce-scatter.6.cloned.1.call-done = f32[16,2048]{1,0:T(8,128)} async-done(((f32[128,2048]{1,0:T(8,128)}), f32[16,2048]{1,0:T(8,128)}) %reduce-scatter.6.cloned.1.call-update) | async-done | bytes 131088 | tf_op jit(solution)/shard_map/reduce_scatter | solution.py:131
  936.2 203.0 %all-gather.3.cloned.1.call-done = f32[1048576]{0:T(1024)} async-done(((f32[2048]{0:T(1024)}), f32[1048576]{0:T(1024)}) %all-gather.3.cloned.1.call-update) | async-done | bytes 4194320 | tf_op jit(solution)/shard_map/all_gather | solution.py:143
  1139.2 5.0 reshape.134
  (86 shorter events, 58.3 us)
Async XLA Ops:
  7.2 254.9 %copy-start = (bf16[1,2048,384]{2,1,0:T(8,128)(2,1)S(1)}, bf16[1,2048,384]{2,1,0:T(8,128)(2,1)}, u32[]{:S(2)}) copy-start(bf16[1,2048,384]{2,1,0:T(8,128)(2,1)} %param.14) | copy-start | bytes 4718596
  46.3 13.8 %copy-start.9 = (s32[128,8]{0,1:T(8,128)S(1)}, s32[128,8]{0,1:T(8,128)}, u32[]{:S(2)}) copy-start(s32[128,8]{0,1:T(8,128)} %param.12) | copy-start | bytes 12292
  46.3 13.9 %copy-start.10 = (f32[128,8]{0,1:T(8,128)S(1)}, f32[128,8]{0,1:T(8,128)}, u32[]{:S(2)}) copy-start(f32[128,8]{0,1:T(8,128)} %param.13) | copy-start | bytes 12292
  46.3 14.2 %copy-start.6 = (bf16[16,2048]{1,0:T(8,128)(2,1)S(1)}, bf16[16,2048]{1,0:T(8,128)(2,1)}, u32[]{:S(2)}) copy-start(bf16[16,2048]{1,0:T(8,128)(2,1)} %param.10) | copy-start | bytes 196612
  46.3 197.3 %all-to-all-start = ((bf16[64,12,2048]{2,1,0:T(8,128)(2,1)}), bf16[64,12,2048]{2,1,0:T(8,128)(2,1)}, u32[]{:S(2)}, u32[]{:S(2)}) async-start(bf16[64,12,2048]{2,1,0:T(8,128)(2,1)} %select_select_fusion), calls=%async_computation | async-start | bytes 8388608 | tf_op jit(solution)/shard_map/all_to_all | solution.py:92
  243.6 196.1 %all-to-all-start.2 = ((bf16[64,12,2048]{2,1,0:T(8,128)(2,1)}), bf16[64,12,2048]{2,1,0:T(8,128)(2,1)}, u32[]{:S(2)}, u32[]{:S(2)}) async-start(bf16[64,12,2048]{2,1,0:T(8,128)(2,1)} %multiply_convert_fusion), calls=%async_computation.3 | async-start | bytes 8388608 | tf_op jit(solution)/shard_map/all_to_all | solution.py:93
  266.4 179.5 %copy-start.4 = (bf16[1,192,2048]{2,1,0:T(8,128)(2,1)S(1)}, bf16[1,192,2048]{2,1,0:T(8,128)(2,1)}, u32[]{:S(2)}) copy-start(bf16[1,192,2048]{2,1,0:T(8,128)(2,1)} %param.15) | copy-start | bytes 2359300
  449.4 0.7 copy-start.11
  449.4 0.8 copy-start.13
  459.8 194.7 %all-to-all-start.3 = ((bf16[64,12,2048]{2,1,0:T(8,128)(2,1)}), bf16[64,12,2048]{2,1,0:T(8,128)(2,1)}, u32[]{:S(2)}, u32[]{:S(2)}) async-start(bf16[64,12,2048]{2,1,0:T(8,128)(2,1)} %reshape.107), calls=%async_computation.4 | async-start | bytes 8388608 | tf_op jit(solution)/shard_map/all_to_all | solution.py:105
  654.5 195.3 %all-to-all-start.1 = ((bf16[64,12,2048]{2,1,0:T(8,128)(2,1)}), bf16[64,12,2048]{2,1,0:T(8,128)(2,1)}, u32[]{:S(2)}, u32[]{:S(2)}) async-start(bf16[64,12,2048]{2,1,0:T(8,128)(2,1)} %reshape.104), calls=%async_computation.1 | async-start | bytes 8388608 | tf_op jit(solution)/shard_map/all_to_all | solution.py:104
  666.4 195.2 %reduce-scatter.8.cloned.1.call-start = ((), (), s32[]{:S(2)}) async-start(), calls=%async_computation.8 | async-start | bytes 1179648 | tf_op jit(solution)/shard_map/reduce_scatter | solution.py:132
  676.4 216.7 %reduce-scatter.10.cloned.1.call-start = ((), (), s32[]{:S(2)}) async-start(), calls=%async_computation.10 | async-start | bytes 73728
  857.6 4.0 copy-start.3
  857.6 4.0 copy-start.8
  858.8 75.8 %reduce-scatter.6.cloned.1.call-start = ((), (), s32[]{:S(2)}) async-start(), calls=%async_computation.7 | async-start | bytes 1179648 | tf_op jit(solution)/shard_map/reduce_scatter | solution.py:131
  861.5 5.5 copy-start.2
  861.6 277.7 %all-gather.3.cloned.1.call-start = ((), (), s32[]{:S(2)}) async-start(), calls=%async_computation.9 | async-start | bytes 4202496 | tf_op jit(solution)/shard_map/all_gather | solution.py:143
  863.4 3.6 copy-start.12
  863.4 3.6 copy-start.14
  867.1 67.5 %copy-start.5 = (f32[16,2048]{1,0:T(8,128)S(1)}, f32[16,2048]{1,0:T(8,128)}, u32[]{:S(2)}) copy-start(f32[16,2048]{1,0:T(8,128)} %reduce-scatter.8.cloned.1.call-done) | copy-start | bytes 393220
  867.1 67.5 %copy-start.7 = (bf16[16,2048]{1,0:T(8,128)(2,1)S(1)}, bf16[16,2048]{1,0:T(8,128)(2,1)}, u32[]{:S(2)}) copy-start(bf16[16,2048]{1,0:T(8,128)(2,1)} %param.10) | copy-start | bytes 196612
  1139.2 8.0 copy-start.1
Sparse Core Ops, SparseCore 0:
  676.5 39.7 reduce-scatter.7
  858.9 34.1 reduce-scatter.9
  896.2 38.3 reduce-scatter.5
  940.4 198.7 all-gather.2
